TPU v7x, 512 devices: a whole 4x4x16 slice. The times are simulated.
512 devices in a mesh: seq: 128 (over z, y, core), ch: 4 (over x).
Axes of the slice: x: 4, y: 4, z: 16, core: 2. Of those that a mesh axis runs over, the one named last changes fastest.
Arguments:
- ingest: bfloat16 [131072, 4096], P('seq', 'ch'), may hold values from -6 to 6
- ingest_count: int32 [128], P('seq'), may hold values from 0 to 1024, as said below
- doc_lengths: int32 [128], replicated, may hold values from 1 to 2048, as said below
- in_weight: bfloat16 [4096, 5120], P('seq', 'ch'), may hold values from -0.09375 to 0.09375
- conv_weight: float32 [4, 5120], P(None, 'ch'), may hold values from -3 to 3
- conv_bias: float32 [5120], P('ch'), may hold values from -3 to 3
Outputs:
- conv_out: bfloat16 [65536, 5120], P('seq', 'ch')
Inputs may be any that keep to these rules, and one draw needn't show every extreme that they name: Device i keeps its valid rows in its first ingest_count[i] slots; the devices before i together hold between i * 512 - 256 and i * 512 + 256 rows, both ends reached in every draw; the first device holds 511 rows, and all devices together hold 65536 rows. `doc_lengths`: the lengths sum to 65536; the first document has exactly 2048 tokens.
All inputs are finite; a program needn't handle non-finite values.
Results may differ from a plain program's by a relative error of at most 0.012.
Values may be sent and summed in bfloat16 or wider, within the bound.
A program may use at most 128 MiB of HBM per device.

v0:
```python
import jax
import jax.numpy as jnp
from jax import lax
from jax.sharding import PartitionSpec as P


def shifted(value, axis, steps):
    count = lax.axis_size(axis)
    initial, last = (max(0, -steps), min(count, count - steps))
    return lax.ppermute(value, axis, [(source, source + steps) for source in range(initial, last)])


def carried_in(value, axis, join, neutral):
    count, mine = (lax.axis_size(axis), lax.axis_index(axis))
    pieces = lax.all_gather(value, axis)
    subtotal = jnp.full_like(value, 0) + jnp.asarray(neutral, value.dtype)

    def turn(position, subtotal):
        longer = join(subtotal, pieces[position])
        return jnp.where(position < mine, longer, subtotal)

    return lax.fori_loop(0, count - 1, turn, subtotal)


def move_rows(ingest, count, offset, first, tokens, extra):
    half = tokens // 2
    slots = ingest.shape[0]
    start = first + tokens - offset - extra
    tail = lax.dynamic_slice_in_dim(ingest, start, half + extra, 0)
    from_left = shifted(tail, "seq", 1)
    from_right = shifted(ingest[:half], "seq", -1)
    next_offset = offset + count
    buffer = jnp.concatenate([from_left, ingest, from_right], axis=0)
    places = first - extra + jnp.arange(tokens + extra, dtype=jnp.int32)
    lead = half + extra
    picks = jnp.where(
        places < offset,
        places - (first - extra),
        jnp.where(
            places < next_offset, lead + places - offset, lead + slots + places - next_offset
        ),
    )
    return jnp.take(buffer, picks.astype(jnp.int32), axis=0)


def body(ingest, ingest_count, doc_lengths, in_weight, conv_weight, conv_bias):
    tokens = ingest.shape[0] // 2
    channels = in_weight.shape[1]
    before = carried_in(
        ingest_count, "seq", lambda earlier, later: earlier + later, jnp.zeros_like(ingest_count)
    )
    offset = before[0]
    count = ingest_count[0]
    first = lax.axis_index("seq") * tokens
    extra = 3
    moved = move_rows(ingest, count, offset, first, tokens, extra)
    features = lax.all_gather(moved, "ch", axis=1, tiled=True)
    window = jnp.dot(
        features,
        lax.all_gather(in_weight, "seq", axis=0, tiled=True),
        preferred_element_type=jnp.float32,
    ).astype(jnp.bfloat16)
    values = window.astype(jnp.float32)
    starts = jnp.cumsum(doc_lengths) - doc_lengths
    places = first - 3 + jnp.arange(tokens + 3, dtype=jnp.int32)
    doc_ids = jnp.sum((places[:, None] >= starts[None, :]).astype(jnp.int32), axis=1) - 1
    here_ids = doc_ids[3:]
    total = jnp.zeros((tokens, channels), jnp.float32) + conv_bias[None, :]
    for lag in range(4):
        earlier = values[3 - lag : 3 - lag + tokens]
        same = (doc_ids[3 - lag : 3 - lag + tokens] == here_ids).astype(jnp.float32)
        total = total + conv_weight[lag][None, :] * earlier * same[:, None]
    return jax.nn.silu(total).astype(jnp.bfloat16)


def solution(mesh):
    placed = (P("seq", "ch"), P("seq"), P(), P("seq", "ch"), P(None, "ch"), P("ch"))
    return jax.shard_map(
        body, mesh=mesh, in_specs=placed, out_specs=P("seq", "ch"), check_vma=False
    )
```

profile of v0, /device:TPU:1, one launch (start us, length us, event | category | flops | bytes accessed | tf_op | source)
XLA Modules:
  0.0 486.9 jit_solution(12569060451620937295)
XLA Ops:
  7.2 1.3 dynamic-slice
  8.5 0.8 dynamic-update-slice
  9.2 30.5 %all-reduce = s32[128]{0:T(128)S(1)} all-reduce(s32[128]{0:T(128)S(1)} %dynamic-update-slice), channel_id=2, replica_groups=mesh['seq'=128,'ch'=4] {'seq'}, use_global_device_ids=true, to_apply=%add | all-reduce | flops 128 | bytes 1024
  39.7 175.2 %while.13 = (s32[]{:T(128)}, s32[1]{0:T(128)}, s32[]{:T(128)}, s32[128,1]{0,1:T(1,128)S(1)}, s32[]{:T(128)}) while((s32[]{:T(128)}, s32[1]{0:T(128)}, s32[]{:T(128)}, s32[128,1]{0,1:T(1,128)S(1)}, s32[]{:T(128)}) %tuple.40), condition=%wide.region_1.2_spmd, body=%wide.region_0.1_spmd.sunk | while | flops 5 | bytes 107 | solution.py:22
  41.1 0.7 constant_dynamic-slice_fusion.3
  42.5 0.7 constant_dynamic-slice_fusion.3
  43.9 0.7 constant_dynamic-slice_fusion.3
  45.3 0.7 constant_dynamic-slice_fusion.3
  46.6 0.7 constant_dynamic-slice_fusion.3
  48.0 0.7 constant_dynamic-slice_fusion.3
  49.4 0.7 constant_dynamic-slice_fusion.3
  50.8 0.7 constant_dynamic-slice_fusion.3
  52.2 0.7 constant_dynamic-slice_fusion.3
  53.5 0.7 constant_dynamic-slice_fusion.3
  54.9 0.7 constant_dynamic-slice_fusion.3
  56.3 0.7 constant_dynamic-slice_fusion.3
  57.7 0.7 constant_dynamic-slice_fusion.3
  59.1 0.7 constant_dynamic-slice_fusion.3
  215.0 1.2 constant_dynamic-slice_fusion.1
  216.2 7.4 %collective-permute-start = (bf16[259,1024]{1,0:T(8,128)(2,1)S(1)}, bf16[259,1024]{1,0:T(8,128)(2,1)}, u32[]{:S(2)}, u32[]{:S(2)}) collective-permute-start(bf16[259,1024]{1,0:T(8,128)(2,1)S(1)} %constant_dynamic-slice_fusion.1), channel_id=1, source_target_pairs={{0,4},{4,8},{8,12},{12,16},{16,20},{20,24},{24,28},{28,32},{32,36}... | collective-permute-start | bytes 1591304 | tf_op jit(solution)/shard_map/ppermute | solution.py:10
  223.6 1.1 slice.41
  224.7 2.2 collective-permute-start.1
  227.0 8.2 %collective-permute-done.1 = bf16[256,1024]{1,0:T(8,128)(2,1)S(1)} collective-permute-done((bf16[256,1024]{1,0:T(8,128)(2,1)S(1)}, bf16[256,1024]{1,0:T(8,128)(2,1)S(1)}, u32[]{:S(2)}, u32[]{:S(2)}) %collective-permute-start.1) | collective-permute-done | bytes 524320 | tf_op jit(solution)/shard_map/ppermute | solution.py:10
  235.2 0.8 copy-done
  236.0 14.8 %concatenate.3 = bf16[1539,1024]{1,0:T(8,128)(2,1)S(1)} concatenate(bf16[259,1024]{1,0:T(8,128)(2,1)} %collective-permute-done, bf16[1024,1024]{1,0:T(8,128)(2,1)} %param.8, bf16[256,1024]{1,0:T(8,128)(2,1)} %copy-done), dimensions={0} | concatenate | bytes 6303744 | tf_op jit(solution)/shard_map/concatenate | solution.py:33
  250.8 3.4 gather_fusion
  254.1 2.4 broadcast_select_fusion
  256.6 0.7 all-gather.6.cloned.1.call-update
  258.2 52.7 %all-gather.4.cloned.1.call-done = bf16[515,4096]{1,0:T(8,128)(2,1)} async-done(((bf16[515,1024]{1,0:T(8,128)(2,1)}), bf16[515,4096]{1,0:T(8,128)(2,1)}) %all-gather.4.cloned.1.call-update) | async-done | bytes 4218896 | tf_op jit(solution)/shard_map/all_gather | solution.py:57
  310.8 154.9 %all-gather.6.cloned.1.call-done = bf16[4096,1280]{1,0:T(8,128)(2,1)} async-done(((bf16[32,1280]{1,0:T(8,128)(2,1)}), bf16[4096,1280]{1,0:T(8,128)(2,1)}) %all-gather.6.cloned.1.call-update) | async-done | bytes 10485776 | tf_op jit(solution)/shard_map/all_gather | solution.py:60
  465.8 10.9 %fusion = f32[515,1280]{1,0:T(8,128)S(1)} fusion(bf16[515,4096]{1,0:T(8,128)(2,1)} %all-gather.4.cloned.1.call-done, bf16[4096,1280]{1,0:T(8,128)(2,1)} %all-gather.6.cloned.1.call-done), kind=kOutput, calls=%fused_computation.3 | convolution fusion | flops 5401485312 | bytes 17341440 | tf_op jit(solution)/shard_map/dot_general | solution.py:58
  476.7 3.3 multiply_convert_fusion
  (137 shorter events, 76.0 us)
Async XLA Ops:
  6.5 304.3 %all-gather.4.cloned.1.call-start = ((), (), s32[]{:S(2)}) async-start(), calls=%async_computation | async-start | bytes 5324800 | tf_op jit(solution)/shard_map/all_gather | solution.py:57
  216.2 19.8 %collective-permute-start = (bf16[259,1024]{1,0:T(8,128)(2,1)S(1)}, bf16[259,1024]{1,0:T(8,128)(2,1)}, u32[]{:S(2)}, u32[]{:S(2)}) collective-permute-start(bf16[259,1024]{1,0:T(8,128)(2,1)S(1)} %constant_dynamic-slice_fusion.1), channel_id=1, source_target_pairs={{0,4},{4,8},{8,12},{12,16},{16,20},{20,24},{24,28},{28,32},{32,36}... | collective-permute-start | bytes 1591304 | tf_op jit(solution)/shard_map/ppermute | solution.py:10
  224.7 10.5 %collective-permute-start.1 = (bf16[256,1024]{1,0:T(8,128)(2,1)S(1)}, bf16[256,1024]{1,0:T(8,128)(2,1)S(1)}, u32[]{:S(2)}, u32[]{:S(2)}) collective-permute-start(bf16[256,1024]{1,0:T(8,128)(2,1)S(1)} %slice.41), channel_id=1, source_target_pairs={{4,0},{8,4},{12,8},{16,12},{20,16},{24,20},{28,24},{32,28},{36,32}... | collective-permute-start | bytes 1572872 | tf_op jit(solution)/shard_map/ppermute | solution.py:10
  235.2 0.8 copy-start
  254.1 3.2 copy-start.3
  254.1 3.9 copy-start.1
  256.6 209.2 %all-gather.6.cloned.1.call-start = ((), (), s32[]{:S(2)}) async-start(), calls=%async_computation.1 | async-start | bytes 10567680 | tf_op jit(solution)/shard_map/all_gather | solution.py:60
  258.2 218.6 %copy-start.2 = (f32[1280]{0:T(1024)S(1)}, f32[1280]{0:T(1024)}, u32[]{:S(2)}) copy-start(f32[1280]{0:T(1024)} %param.13) | copy-start | bytes 15364
Sparse Core Ops, SparseCore 0:
  256.7 54.0 all-gather.3
  313.9 151.7 all-gather.5
where the time goes:
time: 489 us; the launch traced here: 487 us
  waiting for transfers between devices  217 us (44%)
  local copies, waits for them, and re-layouts  108 us (22%)
  loops' own time  90.8 us (19%)
  blocking collectives  30.5 us (6%)
  between operations  14.2 us (3%)
  matrix products  10.9 us (2%)
  starting transfers between devices  9.63 us (2%)
  other arithmetic  6.33 us (1%)
    all_gather x1, waiting for transfers between devices, body(): lax.all_gather(in_weight, 'seq', axis=0, tiled=True)  155 us
    another operation x1, loops' own time, carried_in(): return lax.fori_loop(0, count - 1, turn, subtotal)  90.8 us
    dynamic_slice x127, local copies, waits for them, and re-layouts, turn(): longer = join(subtotal, pieces[position])  84.4 us
    all_gather x1, waiting for transfers between devices, body(): features = lax.all_gather(moved, 'ch', axis=1, tiled=True)  52.7 us
    unnamed x1, blocking collectives  30.5 us
    concatenate x1, local copies, waits for them, and re-layouts, move_rows(): buffer = jnp.concatenate([from_left, ingest, from_right], axis=0)  14.8 us
    dot_general x1, matrix products, body(): jnp.dot(features, lax.all_gather(in_weight, 'seq', axis=0, tiled=True), p...  10.9 us
  transfers between devices with their start and end apart: 4, of which 3 were waited for; matrix products, arithmetic and copies ran while one was open for 0% of the time, Pallas kernels for 0%

commit v1 on v0

--- a/solution.py
+++ b/solution.py
@@ -54,7 +54,12 @@
     first = lax.axis_index("seq") * tokens
     extra = 3
     moved = move_rows(ingest, count, offset, first, tokens, extra)
-    features = lax.all_gather(moved, "ch", axis=1, tiled=True)
+    ring = [moved]
+    for hop in range(3):
+        ring.append(lax.ppermute(ring[-1], "ch", [(dev, (dev + 1) % 4) for dev in range(4)]))
+    features = jnp.roll(
+        jnp.concatenate(ring[::-1], axis=1), (lax.axis_index("ch") + 1) * ring[0].shape[1], axis=1
+    )
     window = jnp.dot(
         features,
         lax.all_gather(in_weight, "seq", axis=0, tiled=True),

time: 489 us -> 339 us (0.69)
  the two profiles are of different devices: /device:TPU:1 before, /device:TPU:8 now
where the time goes in v1:
time: 339 us; the launch traced here: 337 us
  local copies, waits for them, and re-layouts  101 us (30%)
  waiting for transfers between devices  84 us (25%)
  loops' own time  72.9 us (22%)
  blocking collectives  33.3 us (10%)
  between operations  14.3 us (4%)
  starting transfers between devices  13.1 us (4%)
  matrix products  11 us (3%)
  other arithmetic  7.86 us (2%)
    ppermute x3, waiting for transfers between devices, body(): lax.ppermute(ring[-1], 'ch', [(dev, (dev + 1) % 4) for dev in range(4)])  76.7 us
    another operation x1, loops' own time, carried_in(): return lax.fori_loop(0, count - 1, turn, subtotal)  72.9 us
    dynamic_slice x127, local copies, waits for them, and re-layouts, turn(): longer = join(subtotal, pieces[position])  70.7 us
    unnamed x1, blocking collectives  33.3 us
    concatenate x1, local copies, waits for them, and re-layouts, move_rows(): buffer = jnp.concatenate([from_left, ingest, from_right], axis=0)  14.8 us
    dot_general x1, matrix products, body(): jnp.dot(features, lax.all_gather(in_weight, 'seq', axis=0, tiled=True), p...  11 us
    unnamed x19, local copies, waits for them, and re-layouts  9.25 us
    ppermute x3, starting transfers between devices, body(): lax.ppermute(ring[-1], 'ch', [(dev, (dev + 1) % 4) for dev in range(4)])  7.51 us
  transfers between devices with their start and end apart: 6, of which 4 were waited for; matrix products, arithmetic and copies ran while one was open for 31% of the time, Pallas kernels for 0%

profile of v1, /device:TPU:8, one launch (start us, length us, event | category | flops | bytes accessed | tf_op | source)
XLA Modules:
  0.0 336.9 jit_solution(3772194147720169817)
XLA Ops:
  6.5 0.7 all-gather.3.cloned.1.call-update
  7.9 1.2 dynamic-slice
  9.2 0.7 dynamic-update-slice
  9.8 33.3 %all-reduce = s32[128]{0:T(128)S(1)} all-reduce(s32[128]{0:T(128)S(1)} %dynamic-update-slice), channel_id=2, replica_groups=mesh['seq'=128,'ch'=4] {'seq'}, use_global_device_ids=true, to_apply=%add | all-reduce | flops 128 | bytes 1024
  43.1 143.6 %while.13 = (s32[]{:T(128)}, s32[1]{0:T(128)}, s32[]{:T(128)}, s32[128,1]{0,1:T(1,128)S(1)}, s32[]{:T(128)}) while((s32[]{:T(128)}, s32[1]{0:T(128)}, s32[]{:T(128)}, s32[128,1]{0,1:T(1,128)S(1)}, s32[]{:T(128)}) %tuple.38), condition=%wide.region_1.2_spmd, body=%wide.region_0.1_spmd.sunk | while | flops 5 | bytes 107 | solution.py:22
  46.5 0.6 constant_dynamic-slice_fusion.3
  49.9 0.6 constant_dynamic-slice_fusion.3
  186.7 1.2 constant_dynamic-slice_fusion.1
  187.9 1.9 collective-permute-start
  189.8 1.1 slice.41
  190.9 3.6 %collective-permute-start.1 = (bf16[256,1024]{1,0:T(8,128)(2,1)S(1)}, bf16[256,1024]{1,0:T(8,128)(2,1)S(1)}, u32[]{:S(2)}, u32[]{:S(2)}) collective-permute-start(bf16[256,1024]{1,0:T(8,128)(2,1)S(1)} %slice.41), channel_id=1, source_target_pairs={{4,0},{8,4},{12,8},{16,12},{20,16},{24,20},{28,24},{32,28},{36,32}... | collective-permute-start | bytes 1572872 | tf_op jit(solution)/shard_map/ppermute | solution.py:10
  194.6 6.6 %collective-permute-done.1 = bf16[256,1024]{1,0:T(8,128)(2,1)S(1)} collective-permute-done((bf16[256,1024]{1,0:T(8,128)(2,1)S(1)}, bf16[256,1024]{1,0:T(8,128)(2,1)S(1)}, u32[]{:S(2)}, u32[]{:S(2)}) %collective-permute-start.1) | collective-permute-done | bytes 524320 | tf_op jit(solution)/shard_map/ppermute | solution.py:10
  201.2 0.8 copy-done.1
  202.0 14.8 %concatenate.9 = bf16[1539,1024]{1,0:T(8,128)(2,1)S(1)} concatenate(bf16[259,1024]{1,0:T(8,128)(2,1)} %collective-permute-done, bf16[1024,1024]{1,0:T(8,128)(2,1)} %param.8, bf16[256,1024]{1,0:T(8,128)(2,1)} %copy-done.1), dimensions={0} | concatenate | bytes 6303744 | tf_op jit(solution)/shard_map/concatenate | solution.py:33
  216.9 3.4 gather_fusion
  220.2 1.4 broadcast_select_fusion
  221.6 3.4 %collective-permute-start.2 = (bf16[515,1024]{1,0:T(8,128)(2,1)S(1)}, bf16[515,1024]{1,0:T(8,128)(2,1)S(1)}, u32[]{:S(2)}, u32[]{:S(2)}) collective-permute-start(bf16[515,1024]{1,0:T(8,128)(2,1)S(1)} %broadcast_select_fusion), channel_id=1, source_target_pairs={{0,1},{1,2},{2,3},{3,0},{4,5},{5,6},{6,7},{7,4},{8,9},{9,10},{10,1... | collective-permute-start | bytes 3164168 | tf_op jit(solution)/shard_map/ppermute | solution.py:59
  225.1 25.8 %collective-permute-done.2 = bf16[515,1024]{1,0:T(8,128)(2,1)S(1)} collective-permute-done((bf16[515,1024]{1,0:T(8,128)(2,1)S(1)}, bf16[515,1024]{1,0:T(8,128)(2,1)S(1)}, u32[]{:S(2)}, u32[]{:S(2)}) %collective-permute-start.2) | collective-permute-done | bytes 1054752 | tf_op jit(solution)/shard_map/ppermute | solution.py:59
  250.9 2.2 collective-permute-start.3
  253.1 26.2 %collective-permute-done.3 = bf16[515,1024]{1,0:T(8,128)(2,1)S(1)} collective-permute-done((bf16[515,1024]{1,0:T(8,128)(2,1)S(1)}, bf16[515,1024]{1,0:T(8,128)(2,1)S(1)}, u32[]{:S(2)}, u32[]{:S(2)}) %collective-permute-start.3) | collective-permute-done | bytes 1054752 | tf_op jit(solution)/shard_map/ppermute | solution.py:59
  279.2 1.9 collective-permute-start.4
  282.0 24.7 %collective-permute-done.4 = bf16[515,1024]{1,0:T(8,128)(2,1)S(1)} collective-permute-done((bf16[515,1024]{1,0:T(8,128)(2,1)S(1)}, bf16[515,1024]{1,0:T(8,128)(2,1)S(1)}, u32[]{:S(2)}, u32[]{:S(2)}) %collective-permute-start.4) | collective-permute-done | bytes 1054752 | tf_op jit(solution)/shard_map/ppermute | solution.py:59
  306.7 1.1 constant_dynamic-update-slice_fusion.7
  307.8 1.1 constant_dynamic-update-slice_fusion.6
  308.9 1.1 constant_dynamic-update-slice_fusion.5
  310.0 1.3 constant_dynamic-update-slice_fusion.4
  311.3 1.1 constant_dynamic-update-slice_fusion.3
  312.3 1.1 constant_dynamic-update-slice_fusion.2
  313.5 1.1 constant_dynamic-update-slice_fusion.1
  314.5 1.3 constant_dynamic-update-slice_fusion
  315.8 11.0 %fusion.5 = f32[515,1280]{1,0:T(8,128)S(1)} fusion(bf16[4096,1280]{1,0:T(8,128)(2,1)} %all-gather.3.cloned.1.call-done, bf16[515,8192]{1,0:T(8,128)(2,1)} %constant_dynamic-update-slice_fusion, s32[]{:T(128)S(6)} %select_n.92), kind=kOutput, calls=%fused_computation.5 | convolution fusion | flops 5401485312 | bytes 17382404 | tf_op jit(solution)/shard_map/dot_general | solution.py:63
  326.8 3.3 multiply_convert_fusion
  (150 shorter events, 70.5 us)
Async XLA Ops:
  6.5 309.3 %all-gather.3.cloned.1.call-start = ((), (), s32[]{:S(2)}) async-start(), calls=%async_computation | async-start | bytes 10567680 | tf_op jit(solution)/shard_map/all_gather | solution.py:65
  187.9 14.1 %collective-permute-start = (bf16[259,1024]{1,0:T(8,128)(2,1)S(1)}, bf16[259,1024]{1,0:T(8,128)(2,1)}, u32[]{:S(2)}, u32[]{:S(2)}) collective-permute-start(bf16[259,1024]{1,0:T(8,128)(2,1)S(1)} %constant_dynamic-slice_fusion.1), channel_id=1, source_target_pairs={{0,4},{4,8},{8,12},{12,16},{16,20},{20,24},{24,28},{28,32},{32,36}... | collective-permute-start | bytes 1591304 | tf_op jit(solution)/shard_map/ppermute | solution.py:10
  190.9 10.3 %collective-permute-start.1 = (bf16[256,1024]{1,0:T(8,128)(2,1)S(1)}, bf16[256,1024]{1,0:T(8,128)(2,1)S(1)}, u32[]{:S(2)}, u32[]{:S(2)}) collective-permute-start(bf16[256,1024]{1,0:T(8,128)(2,1)S(1)} %slice.41), channel_id=1, source_target_pairs={{4,0},{8,4},{12,8},{16,12},{20,16},{24,20},{28,24},{32,28},{36,32}... | collective-permute-start | bytes 1572872 | tf_op jit(solution)/shard_map/ppermute | solution.py:10
  201.2 0.8 copy-start.1
  216.8 64.3 %copy-start.4 = (s32[128]{0:T(128)S(1)}, s32[128]{0:T(128)}, u32[]{:S(2)}) copy-start(s32[128]{0:T(128)} %param.10) | copy-start | bytes 1540
  216.9 65.0 %copy-start.2 = (f32[4,1280]{1,0:T(4,128)S(1)}, f32[4,1280]{1,0:T(4,128)}, u32[]{:S(2)}) copy-start(f32[4,1280]{1,0:T(4,128)} %param.12) | copy-start | bytes 61444
  221.6 29.2 %collective-permute-start.2 = (bf16[515,1024]{1,0:T(8,128)(2,1)S(1)}, bf16[515,1024]{1,0:T(8,128)(2,1)S(1)}, u32[]{:S(2)}, u32[]{:S(2)}) collective-permute-start(bf16[515,1024]{1,0:T(8,128)(2,1)S(1)} %broadcast_select_fusion), channel_id=1, source_target_pairs={{0,1},{1,2},{2,3},{3,0},{4,5},{5,6},{6,7},{7,4},{8,9},{9,10},{10,1... | collective-permute-start | bytes 3164168 | tf_op jit(solution)/shard_map/ppermute | solution.py:59
  250.9 28.4 %collective-permute-start.3 = (bf16[515,1024]{1,0:T(8,128)(2,1)S(1)}, bf16[515,1024]{1,0:T(8,128)(2,1)S(1)}, u32[]{:S(2)}, u32[]{:S(2)}) collective-permute-start(bf16[515,1024]{1,0:T(8,128)(2,1)S(1)} %collective-permute-done.2), channel_id=1, source_target_pairs={{0,1},{1,2},{2,3},{3,0},{4,5},{5,6},{6,7},{7,4},{8,9},{9,10},{10,1... | collective-permute-start | bytes 3164168 | tf_op jit(solution)/shard_map/ppermute | solution.py:59
  279.2 27.5 %collective-permute-start.4 = (bf16[515,1024]{1,0:T(8,128)(2,1)S(1)}, bf16[515,1024]{1,0:T(8,128)(2,1)S(1)}, u32[]{:S(2)}, u32[]{:S(2)}) collective-permute-start(bf16[515,1024]{1,0:T(8,128)(2,1)S(1)} %collective-permute-done.3), channel_id=1, source_target_pairs={{0,1},{1,2},{2,3},{3,0},{4,5},{5,6},{6,7},{7,4},{8,9},{9,10},{10,1... | collective-permute-start | bytes 3164168 | tf_op jit(solution)/shard_map/ppermute | solution.py:59
  307.8 2.2 copy-start
  315.8 11.0 %copy-start.3 = (f32[1280]{0:T(1024)S(1)}, f32[1280]{0:T(1024)}, u32[]{:S(2)}) copy-start(f32[1280]{0:T(1024)} %param.13) | copy-start | bytes 15364
Sparse Core Ops, SparseCore 0:
  10.5 152.7 all-gather.2
